TPU v7x, 128 devices: a whole 4x4x4 slice. The times are simulated.
128 devices in a mesh: tensor: 8 (over x_hi, y), seq: 16 (over z, x_lo, core).
Axes of the slice: x: 4 (x_hi: 2, x_lo: 2; x = x_hi * 2 + x_lo), y: 4, z: 4, core: 2. Of those that a mesh axis runs over, the one named last changes fastest.
Arguments:
- teacher_query: bfloat16 [6144, 4096], P('seq', 'tensor'), may hold values from -9 to 9
- teacher_keys: bfloat16 [6144, 1024], P('seq', 'tensor'), may hold values from -6 to 6
- teacher_values: bfloat16 [6144, 1024], P('seq', 'tensor'), may hold values from -24 to 24
- out_proj: bfloat16 [4096, 8192], P('tensor'), may hold values from -0.1875 to 0.1875
- teacher_stream: bfloat16 [6144, 8192], P('seq', 'tensor'), may hold values from -6 to 6
- student_stream: bfloat16 [6144, 4096], P('seq', 'tensor'), may hold values from -400 to 400
- student_gain: float32 [4096], replicated, may hold values from 0.25 to 1.75
- distill_proj: bfloat16 [4096, 8192], P('seq', 'tensor'), may hold values from -0.09375 to 0.09375
- token_mask: int32 [6144], P('seq'), may hold values 0 or 1
Outputs:
- grad_distill: bfloat16 [4096, 8192], P('seq', 'tensor')
- grad_stream: float32 [6144, 4096], P('seq', 'tensor')
All inputs are finite; a program needn't handle non-finite values. No bound on the sum of `token_mask` on one device may be relied on, other than what follows from the above.
Results may differ from a plain program's by a relative error of at most 0.024.
Values may be sent and summed in bfloat16 or wider, within the bound.
A program may use at most 192 MiB of HBM per device.

v0:
```python
import math

import jax
import jax.numpy as jnp
from jax import lax
from jax.sharding import PartitionSpec as P

Q_HEADS = 32
KV_HEADS = 8
HEAD_DIM = 128


masked_score = -1e30
norm_eps = 1e-05


def body(
    teacher_query,
    teacher_keys,
    teacher_values,
    out_proj,
    teacher_stream,
    student_stream,
    student_gain,
    distill_proj,
    token_mask,
):
    row_count = teacher_query.shape[0]
    head_local = teacher_keys.shape[1] // HEAD_DIM
    group_size = Q_HEADS // KV_HEADS
    score_scale = 1.0 / math.sqrt(HEAD_DIM)
    total_tokens = row_count * lax.axis_size("seq")
    query_total = group_size * row_count
    queries = (
        teacher_query.reshape(row_count, head_local, group_size, HEAD_DIM)
        .transpose(1, 2, 0, 3)
        .reshape(head_local, query_total, HEAD_DIM)
    )
    query_rows = jnp.tile(
        lax.axis_index("seq") * row_count + jnp.arange(row_count, dtype=jnp.int32), group_size
    )
    keys_block = lax.all_gather(teacher_keys, "seq", axis=0, tiled=True)
    values_block = lax.all_gather(teacher_values, "seq", axis=0, tiled=True)
    block_len = keys_block.shape[0]
    keys_heads = keys_block.reshape(block_len, head_local, HEAD_DIM)
    values_heads = values_block.reshape(block_len, head_local, HEAD_DIM)
    scores = (
        jnp.einsum("hqd,khd->hqk", queries, keys_heads, preferred_element_type=jnp.float32)
        * score_scale
    )
    allowed = query_rows[:, None] >= jnp.arange(block_len, dtype=jnp.int32)[None, :]
    scores = jnp.where(allowed, scores, masked_score)
    running_max = jnp.full((head_local, query_total), masked_score, jnp.float32)
    new_max = jnp.maximum(running_max, jnp.max(scores, axis=-1))
    weights = jnp.where(allowed, jnp.exp(scores - new_max[..., None]), 0.0)
    totals = jnp.sum(weights, axis=-1)
    context_sum = jnp.einsum(
        "hqk,khd->hqd",
        weights.astype(jnp.bfloat16),
        values_heads,
        preferred_element_type=jnp.float32,
    )
    running_max, totals, context_sum = (new_max, totals, context_sum)
    context = (context_sum / totals[..., None]).reshape(head_local, group_size, row_count, HEAD_DIM)
    context = (
        context.transpose(2, 0, 1, 3)
        .reshape(row_count, head_local * group_size * HEAD_DIM)
        .astype(jnp.bfloat16)
    )
    partial_out = jnp.dot(context, out_proj, preferred_element_type=jnp.float32)
    teacher_out = lax.psum_scatter(
        partial_out.astype(jnp.bfloat16), "tensor", scatter_dimension=1, tiled=True
    ).astype(jnp.float32)
    target = (teacher_stream.astype(jnp.float32) + teacher_out).astype(jnp.bfloat16)
    proj_full = lax.all_gather(distill_proj, "seq", axis=0, tiled=True)
    own_cols = student_stream.shape[1]
    first_col = lax.axis_index("tensor") * own_cols
    hidden_full = lax.all_gather(student_stream, "tensor", axis=1, tiled=True).astype(jnp.float32)
    inverse = lax.rsqrt(jnp.mean(hidden_full * hidden_full, axis=-1, keepdims=True) + norm_eps)
    scaled_rows = hidden_full * inverse
    normed = (scaled_rows * student_gain).astype(jnp.bfloat16)
    predicted = jnp.dot(normed, proj_full, preferred_element_type=jnp.float32)
    mismatch = token_mask.astype(jnp.float32)[:, None] * (predicted - target.astype(jnp.float32))
    mismatch_half = mismatch.astype(jnp.bfloat16)
    inv_scale = 1.0 / math.sqrt(total_tokens)
    grad_distill = lax.psum_scatter(
        (
            lax.dot_general(
                normed, mismatch_half, (((0,), (0,)), ((), ())), preferred_element_type=jnp.float32
            )
            * inv_scale
        ).astype(jnp.bfloat16),
        "seq",
        scatter_dimension=0,
        tiled=True,
    )
    normed_terms = lax.dot_general(
        mismatch_half, proj_full, (((1,), (1,)), ((), ())), preferred_element_type=jnp.float32
    )
    normed_grad = lax.psum(normed_terms.astype(jnp.bfloat16), "tensor").astype(jnp.float32)
    gained = normed_grad * student_gain
    inner_mean = jnp.mean(gained * scaled_rows, axis=-1, keepdims=True)
    grad_full = inverse * (gained - scaled_rows * inner_mean)
    grad_stream = lax.dynamic_slice_in_dim(grad_full, first_col, own_cols, 1)
    return (grad_distill, grad_stream)


def solution(mesh):
    placed = (
        P("seq", "tensor"),
        P("seq", "tensor"),
        P("seq", "tensor"),
        P("tensor", None),
        P("seq", "tensor"),
        P("seq", "tensor"),
        P(),
        P("seq", "tensor"),
        P("seq"),
    )
    return jax.shard_map(
        body,
        mesh=mesh,
        in_specs=placed,
        out_specs=(P("seq", "tensor"), P("seq", "tensor")),
        check_vma=False,
    )
```

profile of v0, /device:TPU:0, one launch (start us, length us, event | category | flops | bytes accessed | tf_op | source)
XLA Modules:
  0.0 515.1 jit_solution(15113288769710190411)
XLA Ops:
  7.2 0.7 all-gather.9.cloned.1.call-update
  7.9 0.7 all-gather.11.cloned.1.call-update
  8.7 0.7 all-gather.5.cloned.1.call-update
  9.4 0.5 all-gather.7.cloned.1.call-update
  10.0 1.2 copy.12
  11.3 0.2 copy.13
  11.5 34.0 %all-gather.9.cloned.1.call-done = bf16[6144,128]{1,0:T(8,128)(2,1)} async-done(((bf16[384,128]{1,0:T(8,128)(2,1)}), bf16[6144,128]{1,0:T(8,128)(2,1)}) %all-gather.9.cloned.1.call-update) | async-done | bytes 1572880 | tf_op jit(solution)/shard_map/all_gather | solution.py:42
  45.5 16.0 %fusion = (f32[1536]{0:T(1024)S(1)}, f32[1536,6144]{1,0:T(8,128)}) fusion(s32[1536]{0:T(1024)S(1)} %ge.15, bf16[1536,128]{1,0:T(8,128)(2,1)S(1)} %bitcast.17, bf16[6144,128]{1,0:T(8,128)(2,1)} %all-gather.9.cloned.1.call-done), kind=kOutput, calls=%fused_computation.3 | convolution fusion | flops 2453666304 | bytes 39727104 | tf_op jit(solution)/shard_map/hqd,khd->hqk/dot_general | solution.py:48
  61.5 18.7 %fusion.1 = f32[1536]{0:T(1024)S(1)} fusion(f32[1536,6144]{1,0:T(8,128)} %get-tuple-element.6, f32[1536]{0:T(1024)S(1)} %broadcast_maximum_fusion, s32[1536]{0:T(1024)S(1)} %ge.15), kind=kLoop, calls=%fused_computation.4 | loop fusion | flops 56621568 | bytes 37767168 | tf_op jit(solution)/shard_map/reduce_sum | solution.py:56
  80.2 0.3 all-gather.11.cloned.1.call-done
  80.5 17.4 %fusion.9 = bf16[1536,128]{1,0:T(8,128)(2,1)S(1)} fusion(bf16[6144,128]{1,0:T(8,128)(2,1)} %all-gather.11.cloned.1.call-done, f32[1536,6144]{1,0:T(8,128)} %get-tuple-element.6, f32[1536]{0:T(1024)S(1)} %broadcast_maximum_fusion, s32[1536]{0:T(1024)S(1)} %ge.15, f32[1536]{0:T(1024)S(1)} %fusion.1), kind=kOutput, calls=%fused_computation.17 | convolution fusion | flops 2472935424 | bytes 39733248 | tf_op jit(solution)/shard_map/hqk,khd->hqd/dot_general | solution.py:57
  98.1 9.5 %convolution_convert_fusion = bf16[384,8192]{1,0:T(8,128)(2,1)} fusion(bf16[384,512]{0,1:T(8,128)(2,1)S(1)} %bitcast.16, bf16[512,8192]{1,0:T(8,128)(2,1)} %param.12), kind=kOutput, calls=%fused_computation.8 | convolution fusion | flops 3224371200 | bytes 15073280 | tf_op jit(solution)/shard_map/dot_general | solution.py:70
  107.7 0.6 copy-done.2
  108.3 38.2 %all-gather.5.cloned.1.call-done = bf16[384,4096]{1,0:T(8,128)(2,1)} async-done(((bf16[384,512]{1,0:T(8,128)(2,1)}), bf16[384,4096]{1,0:T(8,128)(2,1)}) %all-gather.5.cloned.1.call-update) | async-done | bytes 3145744 | tf_op jit(solution)/shard_map/all_gather | solution.py:78
  146.6 2.6 fusion.5
  149.2 49.1 %all-gather.7.cloned.1.call-done = bf16[4096,1024]{1,0:T(8,128)(2,1)} async-done(((bf16[256,1024]{1,0:T(8,128)(2,1)}), bf16[4096,1024]{1,0:T(8,128)(2,1)}) %all-gather.7.cloned.1.call-update) | async-done | bytes 8388624 | tf_op jit(solution)/shard_map/all_gather | solution.py:75
  198.3 9.0 %fusion.14 = f32[384,1024]{1,0:T(8,128)} fusion(bf16[4096,1024]{1,0:T(8,128)(2,1)} %all-gather.7.cloned.1.call-done, f32[4096]{0:T(1024)S(1)} %copy-done.1, bf16[384,4096]{1,0:T(8,128)(2,1)} %all-gather.5.cloned.1.call-done, f32[384]{0:T(512)S(1)} %add_rsqrt_fusion), kind=kOutput, calls=%fused_computation.22 | convolution fusion | flops 3227516928 | bytes 13125120 | tf_op jit(solution)/shard_map/dot_general | solution.py:82
  207.2 93.9 %reduce-scatter.3.cloned.1.call-done = bf16[384,1024]{1,0:T(8,128)(2,1)} async-done(((bf16[384,8192]{1,0:T(8,128)(2,1)}), bf16[384,1024]{1,0:T(8,128)(2,1)}) %reduce-scatter.3.cloned.1.call-update) | async-done | bytes 786448 | tf_op jit(solution)/shard_map/reduce_scatter | solution.py:71
  301.1 9.6 %convolution_convert_fusion.1 = bf16[384,4096]{1,0:T(8,128)(2,1)} fusion(bf16[4096,1024]{1,0:T(8,128)(2,1)} %all-gather.7.cloned.1.call-done, f32[384,1024]{1,0:T(8,128)} %fusion.14, f32[384]{0:T(512)S(1)} %convert_element_type.54, bf16[384,1024]{1,0:T(8,128)(2,1)} %reduce-scatter.3.cloned.1.call-done, bf16[384,1024]{1,0:T(8,128)(2,1)} %param.13), kind=kOutput, calls=%fused_computation.15 | convolution fusion | flops 3225944064 | bytes 14681600 | tf_op jit(solution)/shard_map/dot_general | solution.py:97
  310.8 9.2 %multiply_convert_fusion = bf16[4096,1024]{1,0:T(8,128)(2,1)} fusion(f32[384,1024]{1,0:T(8,128)} %fusion.14, f32[4096]{0:T(1024)S(1)} %copy-done.1, f32[384]{0:T(512)S(1)} %convert_element_type.54, bf16[384,1024]{1,0:T(8,128)(2,1)} %reduce-scatter.3.cloned.1.call-done, bf16[384,1024]{1,0:T(8,128)(2,1)} %param.13, bf16[384,4096]{1,0:T(8,128)(2,1)S(1)} %copy-done, ...), kind=kOutput, calls=%fused_computation.7 | convolution fusion | flops 3239051264 | bytes 14699520 | tf_op jit(solution)/shard_map/dot_general | solution.py:88
  320.0 88.5 %all-reduce.2.cloned.1.call-done = bf16[384,4096]{1,0:T(8,128)(2,1)} async-done(((bf16[384,4096]{1,0:T(8,128)(2,1)}), bf16[384,4096]{1,0:T(8,128)(2,1)}) %all-reduce.2.cloned.1.call-update) | async-done | bytes 3145744 | tf_op jit(solution)/shard_map/psum | solution.py:100
  408.6 3.3 multiply_reduce_fusion
  411.9 1.1 fusion.15
  412.9 95.3 %reduce-scatter.5.cloned.1.call-done = bf16[256,1024]{1,0:T(8,128)(2,1)} async-done(((bf16[4096,1024]{1,0:T(8,128)(2,1)}), bf16[256,1024]{1,0:T(8,128)(2,1)}) %reduce-scatter.5.cloned.1.call-update) | async-done | bytes 524304 | tf_op jit(solution)/shard_map/reduce_scatter | solution.py:86
  (23 shorter events, 0.6 us)
Async XLA Ops:
  7.2 38.3 %all-gather.9.cloned.1.call-start = ((), (), s32[]{:S(2)}) async-start(), calls=%async_computation.4 | async-start | bytes 1671168 | tf_op jit(solution)/shard_map/all_gather | solution.py:42
  7.9 72.6 %all-gather.11.cloned.1.call-start = ((), (), s32[]{:S(2)}) async-start(), calls=%async_computation.5 | async-start | bytes 1671168 | tf_op jit(solution)/shard_map/all_gather | solution.py:43
  8.6 137.9 %all-gather.5.cloned.1.call-start = ((), (), s32[]{:S(2)}) async-start(), calls=%async_computation.2 | async-start | bytes 3538944 | tf_op jit(solution)/shard_map/all_gather | solution.py:78
  9.4 188.9 %all-gather.7.cloned.1.call-start = ((), (), s32[]{:S(2)}) async-start(), calls=%async_computation.3 | async-start | bytes 8912896 | tf_op jit(solution)/shard_map/all_gather | solution.py:75
  10.0 291.2 %reduce-scatter.3.cloned.1.call-start = ((), (), s32[]{:S(2)}) async-start(), calls=%async_computation.6 | async-start | bytes 7077888 | tf_op jit(solution)/shard_map/reduce_scatter | solution.py:71
  107.6 0.7 copy-start.2
  107.6 90.6 %copy-start.1 = (f32[4096]{0:T(1024)S(1)}, f32[4096]{0:T(1024)}, u32[]{:S(2)}) copy-start(f32[4096]{0:T(1024)} %param.15) | copy-start | bytes 49156
  107.7 300.9 %all-reduce.2.cloned.1.call-start = ((), (), s32[]{:S(2)}) async-start(), calls=%async_computation.8 | async-start | bytes 6291456 | tf_op jit(solution)/shard_map/psum | solution.py:100
  207.2 103.6 %copy-start = (bf16[384,4096]{1,0:T(8,128)(2,1)S(1)}, bf16[384,4096]{1,0:T(8,128)(2,1)}, u32[]{:S(2)}) copy-start(bf16[384,4096]{1,0:T(8,128)(2,1)} %all-gather.5.cloned.1.call-done) | copy-start | bytes 9437188
  310.8 197.5 %reduce-scatter.5.cloned.1.call-start = ((), (), s32[]{:S(2)}) async-start(), calls=%async_computation.7 | async-start | bytes 8912896 | tf_op jit(solution)/shard_map/reduce_scatter | solution.py:86
Sparse Core Ops, SparseCore 0:
  9.7 35.7 all-gather.8
  47.2 33.2 all-gather.10
  82.7 63.8 all-gather.4
  148.1 50.0 all-gather.6
  201.9 99.1 reduce-scatter.2
  310.9 97.6 all-reduce.1
  411.6 96.6 reduce-scatter.4
where the time goes:
time: 516 us; the launch traced here: 515 us
  waiting for transfers between devices  402 us (78%)
  matrix products  70.6 us (14%)
  other arithmetic  25.7 us (5%)
  between operations  14.2 us (3%)
    reduce_scatter x1, waiting for transfers between devices, body(): lax.psum_scatter((lax.dot_general(normed, mismatch_half, (((0,), (0,)), (...  95.3 us
    reduce_scatter x1, waiting for transfers between devices, body(): lax.psum_scatter(partial_out.astype(jnp.bfloat16), 'tensor', scatter_dime...  93.9 us
    psum x1, waiting for transfers between devices, body(): lax.psum(normed_terms.astype(jnp.bfloat16), 'tensor').astype(jnp.float32)  88.5 us
    all_gather x1, waiting for transfers between devices, body(): proj_full = lax.all_gather(distill_proj, 'seq', axis=0, tiled=True)  49.1 us
    all_gather x1, waiting for transfers between devices, body(): lax.all_gather(student_stream, 'tensor', axis=1, tiled=True)  38.2 us
    all_gather x1, waiting for transfers between devices, body(): keys_block = lax.all_gather(teacher_keys, 'seq', axis=0, tiled=True)  34 us
    reduce_sum x1, other arithmetic, body(): totals = jnp.sum(weights, axis=-1)  18.7 us
    dot_general x1, matrix products, body(): jnp.einsum('hqk,khd->hqd', weights.astype(jnp.bfloat16), values_heads, pr...  17.4 us
  transfers between devices with their start and end apart: 7, of which 7 were waited for; matrix products, arithmetic and copies ran while one was open for 17% of the time, Pallas kernels for 0%

commit v1 on v0

v1 whole, which is shorter than its diff:
```python
import functools
import math

import jax
import jax.numpy as jnp
from jax import lax
from jax.experimental import pallas as pl
from jax.experimental.pallas import tpu as pltpu
from jax.sharding import PartitionSpec as P

HEADS = 4
HEAD_DIM = 128
EPS = 1e-05
ROWS = 384
MASKED = -1e30
MESH = pl.DeviceIdType.MESH
F32 = jnp.float32
BF16 = jnp.bfloat16
SLOTS = 2


def dot(a, b):
    return jnp.dot(a, b, preferred_element_type=F32)


def dot_nt(a, b):
    return lax.dot_general(a, b, (((1,), (1,)), ((), ())), preferred_element_type=F32)


class Copies:
    def __init__(self, send, recv):
        self.send, self.recv = send, recv
        self.started = []

    def make(self, src, dst, k, device):
        return pltpu.make_async_remote_copy(
            src_ref=src, dst_ref=dst, send_sem=self.send.at[k], recv_sem=self.recv.at[k],
            device_id=device, device_id_type=MESH,
        )

    def start(self, src, dst, k, device, again=None):
        self.make(src, dst, k, device).start()
        self.started.append((again or (lambda: src), k, device))

    def arrived(self, ref, k, device):
        self.make(ref, ref, k, device).wait_recv()

    def drain(self):
        for again, k, device in self.started:
            src = again()
            self.make(src, src, k, device).wait_send()
        self.started = []


class Gather:
    def __init__(self, copies, whole, half, near, up, down, ring, pair, other):
        self.c, self.whole, self.half = copies, whole, half
        self.near, self.up, self.down = near, up, down
        self.ring, self.pair, self.other = ring, pair, other

    def at(self, turn, flip):
        r = lax.rem(self.ring + (turn + 4), 4)
        f = 1 - self.pair if flip else self.pair
        return r, f

    def go(self, k, device, place):
        ref = self.whole(*self.at(*place))
        self.c.start(ref, ref, k, device, lambda: self.whole(*self.at(*place)))

    def go_half(self, k, device, place, part):
        ref = self.half(*self.at(*place), part)
        self.c.start(ref, ref, k, device, lambda: self.half(*self.at(*place), part))

    def across(self, k, place):
        if self.other is not None:
            self.go(k, self.other, place)

    def own_near(self):
        self.go(0, self.near, (0, False))

    def own_ring(self):
        self.go(1, self.up, (0, False))
        self.go(2, self.down, (0, False))

    def own_across(self):
        self.across(3, (0, False))

    def got_near(self):
        place = (0, True)
        self.c.arrived(self.whole(*self.at(*place)), 0, self.near)
        self.go(4, self.up, place)
        self.go(5, self.down, place)
        self.across(6, place)

    def got_from_down(self, flip):
        place = (-1, flip)
        self.c.arrived(self.whole(*self.at(*place)), 4 if flip else 1, self.down)
        self.go_half(11 if flip else 7, self.up, place, 0)
        self.across(12 if flip else 8, place)

    def got_from_up(self, flip):
        place = (1, flip)
        self.c.arrived(self.whole(*self.at(*place)), 5 if flip else 2, self.up)
        self.go_half(13 if flip else 9, self.down, place, 1)
        self.across(14 if flip else 10, place)

    def got_far(self, flip):
        place = (2, flip)
        self.c.arrived(self.half(*self.at(*place), 0), 11 if flip else 7, self.down)
        self.c.arrived(self.half(*self.at(*place), 1), 13 if flip else 9, self.up)
        self.across(16 if flip else 15, place)


class Reduce:
    def __init__(self, copies, out, got, near, up, down, ring, pair, base):
        self.c, self.out, self.got = copies, out, got
        self.near, self.up, self.down = near, up, down
        self.ring, self.pair, self.base = ring, pair, base

    def dev(self, k):
        return (self.up, self.down, self.up, self.down, self.up, self.down, self.near)[k]

    def to(self, turn):
        return lax.rem(self.ring + (turn + 4), 4)

    def send(self, j, k, value):
        src = self.out.at[j % SLOTS, k]
        if j >= SLOTS:
            self.c.make(src, src, self.base + (j - SLOTS) * 7 + k, self.dev(k)).wait_send()
        self.out[j % SLOTS, k] = value.astype(BF16)
        self.c.make(src, self.got.at[j, k], self.base + j * 7 + k, self.dev(k)).start()

    def arrived(self, j, k):
        ref = self.got.at[j, k]
        back = (self.down, self.up, self.down, self.up, self.down, self.up, self.near)[k]
        self.c.make(ref, ref, self.base + j * 7 + k, back).wait_recv()

    def load(self, j, k):
        return self.got[j, k].astype(F32)

    def first(self, j, block):
        self.send(j, 0, block(0, self.to(2)))
        self.send(j, 1, block(1, self.to(2)))
        self.send(j, 2, block(1, self.to(1)))
        self.send(j, 3, block(0, self.to(-1)))

    def second(self, j, block):
        self.arrived(j, 0)
        self.send(j, 4, block(0, self.to(1)) + self.load(j, 0))
        self.arrived(j, 1)
        self.send(j, 5, block(1, self.to(-1)) + self.load(j, 1))

    def total(self, j, block, f):
        return block(f, self.ring) + self.load(j, 4 - 2 * f) + self.load(j, 3 + 2 * f)

    def third(self, j, block):
        for k in (2, 3, 4, 5):
            self.arrived(j, k)
        self.send(j, 6, self.total(j, block, 1 - self.pair))

    def last(self, j, block):
        mine = self.total(j, block, self.pair)
        self.arrived(j, 6)
        return mine + self.load(j, 6)

    def drain(self, groups):
        for j in range(max(0, groups - SLOTS), groups):
            for k in range(7):
                src = self.out.at[j % SLOTS, k]
                self.c.make(src, src, self.base + j * 7 + k, self.dev(k)).wait_send()


def kernel(
    q_hbm, k_hbm, v_hbm, op_hbm, ts_ref, ss_hbm, gain_ref, dp_hbm, mask_ref,
    gd_ref, gs_ref,
    q4, kv, dist, stu, normed, normed_t, big, tout, tgot, gout, ggot, sib,
    pred, mm, acc, m_s, l_s, ctx, inv_s, rows_s, ims, imr,
    local, op_sem, kv_s, kv_r, d_s, d_r, s_s, s_r, t_s, t_r, g_s, g_r, b_s, b_r, i_s, i_r,
):
    t, s = lax.axis_index("tensor"), lax.axis_index("seq")
    h, y = lax.div(t, 4), lax.rem(t, 4)
    z, x, c = lax.div(s, 4), lax.rem(lax.div(s, 2), 2), lax.rem(s, 2)
    p = lax.div(s, 2)

    def on_seq(zz, xx, cc):
        return {"tensor": t, "seq": zz * 4 + xx * 2 + cc}

    def on_tensor(hh, yy):
        return {"tensor": hh * 4 + yy, "seq": s}

    z_up, z_down = on_seq(lax.rem(z + 1, 4), x, c), on_seq(lax.rem(z + 3, 4), x, c)
    x_near, sibling = on_seq(z, 1 - x, c), on_seq(z, x, 1 - c)
    y_up, y_down = on_tensor(h, lax.rem(y + 1, 4)), on_tensor(h, lax.rem(y + 3, 4))
    h_near = on_tensor(1 - h, y)

    own_copies = [
        pltpu.make_async_copy(k_hbm, kv.at[0, p, c], local.at[0]),
        pltpu.make_async_copy(v_hbm, kv.at[1, p, c], local.at[1]),
        pltpu.make_async_copy(ss_hbm, stu.at[t], local.at[2]),
        pltpu.make_async_copy(dp_hbm, dist.at[s], local.at[3]),
    ] + [
        pltpu.make_async_copy(q_hbm.at[:, pl.ds(i * HEAD_DIM, HEAD_DIM)], q4.at[i], local.at[4 + i])
        for i in range(HEADS)
    ]
    for copy in own_copies:
        copy.start()

    barrier = pltpu.get_barrier_semaphore()
    for device in (z_up, z_down, x_near, sibling, y_up, y_down, h_near):
        pl.semaphore_signal(barrier, inc=1, device_id=device, device_id_type=MESH)
    pl.semaphore_wait(barrier, 7)

    kv_copies, d_copies, s_copies = Copies(kv_s, kv_r), Copies(d_s, d_r), Copies(s_s, s_r)

    def kv_gather(core):
        return Gather(
            kv_copies, lambda r, f: kv.at[:, r * 2 + f, core], lambda r, f, part: kv.at[part, r * 2 + f, core],
            x_near, z_up, z_down, z, x, sibling,
        )

    def d_gather(core):
        return Gather(
            d_copies, lambda r, f: dist.at[(r * 2 + f) * 2 + core],
            lambda r, f, part: dist.at[(r * 2 + f) * 2 + core, pl.ds(part * 128, 128)],
            x_near, z_up, z_down, z, x, sibling,
        )

    kvg, dg = kv_gather(c), d_gather(c)
    sg = Gather(
        s_copies, lambda r, f: stu.at[f * 4 + r],
        lambda r, f, part: stu.at[f * 4 + r, pl.ds(part * 192, 192)],
        h_near, y_up, y_down, y, h, None,
    )

    def from_sibling(gather, copies, k, turn, flip):
        copies.arrived(gather.whole(*gather.at(turn, flip)), k, sibling)

    kv_other, d_other = kv_gather(1 - c), d_gather(1 - c)

    own_copies[0].wait()
    own_copies[1].wait()
    kvg.own_across()
    kvg.own_near()
    kvg.own_ring()
    own_copies[2].wait()
    sg.own_ring()
    own_copies[3].wait()
    for copy in own_copies[4:]:
        copy.wait()

    def load_out_proj(i, carry):
        for j in range(4):
            start = pl.multiple_of(i * 1024 + j * 256, 256)
            for half in range(2):
                pltpu.make_async_copy(
                    op_hbm.at[pl.ds(half * 256, 256), pl.ds(start, 256)], big.at[j, i, half], op_sem.at[j, i, half]
                ).start()
        return carry

    lax.fori_loop(0, 8, load_out_proj, 0)

    scale = math.log2(math.e) / math.sqrt(HEAD_DIM)

    from_sibling(kv_other, kv_copies, 3, 0, False)
    kk0, vv0 = kv[0, p].reshape(2 * ROWS, HEAD_DIM), kv[1, p].reshape(2 * ROWS, HEAD_DIM)
    visible = (
        lax.broadcasted_iota(jnp.int32, (ROWS, 2 * ROWS), 1)
        <= lax.broadcasted_iota(jnp.int32, (ROWS, 2 * ROWS), 0) + c * ROWS
    )
    for i in range(HEADS):
        scores = jnp.where(visible, dot_nt(q4[i], kk0) * scale, MASKED)
        top = jnp.max(scores, axis=1, keepdims=True)
        weights = jnp.exp2(scores - top)
        m_s[i] = jnp.broadcast_to(top, (ROWS, 128))
        l_s[i] = jnp.broadcast_to(jnp.sum(weights, axis=1, keepdims=True), (ROWS, 128))
        acc[i] = dot(weights.astype(BF16), vv0)

    def step(i, carry):
        @pl.when(i == 1)
        def _():
            kvg.got_near()
            kvg.got_from_down(False)
            kvg.got_from_up(False)
            sg.own_near()
            from_sibling(kv_other, kv_copies, 6, 0, True)

        @pl.when(i == 2)
        def _():
            from_sibling(kv_other, kv_copies, 8, -1, False)
            dg.own_across()
            dg.own_near()
            dg.own_ring()

        @pl.when(i == 3)
        def _():
            from_sibling(kv_other, kv_copies, 10, 1, False)

        @pl.when(i == 4)
        def _():
            kvg.got_from_down(True)
            kvg.got_from_up(True)
            kvg.got_far(False)
            from_sibling(kv_other, kv_copies, 15, 2, False)

        @pl.when(i == 5)
        def _():
            sg.got_near()
            from_sibling(kv_other, kv_copies, 12, -1, True)

        @pl.when(i == 6)
        def _():
            from_sibling(kv_other, kv_copies, 14, 1, True)

        @pl.when(i == 7)
        def _():
            kvg.got_far(True)
            from_sibling(kv_other, kv_copies, 16, 2, True)

        turn = jnp.where(i == 1, 0, jnp.where((i == 2) | (i == 5), 3, jnp.where((i == 3) | (i == 6), 1, 2)))
        flip = jnp.where((i == 1) | (i >= 5), 1 - x, x)
        block = lax.rem(z + turn, 4) * 2 + flip

        @pl.when(block < p)
        def _():
            kk, vv = kv[0, block].reshape(2 * ROWS, HEAD_DIM), kv[1, block].reshape(2 * ROWS, HEAD_DIM)
            for i in range(HEADS):
                scores = dot_nt(q4[i], kk)
                before = m_s[i, :, 0:1]
                top = jnp.maximum(before, jnp.max(scores, axis=1, keepdims=True) * scale)
                weights = jnp.exp2(scores * scale - top)
                fade = jnp.exp2(before - top)
                m_s[i] = jnp.broadcast_to(top, (ROWS, 128))
                l_s[i] = l_s[i] * fade + jnp.sum(weights, axis=1, keepdims=True)
                acc[i] = acc[i] * fade + dot(weights.astype(BF16), vv)

        return carry

    lax.fori_loop(1, 8, step, 0)

    for i in range(HEADS):
        ctx[:, i * HEAD_DIM : (i + 1) * HEAD_DIM] = (acc[i] / l_s[i]).astype(BF16)

    t_copies, g_copies = Copies(t_s, t_r), Copies(g_s, g_r)
    tr = Reduce(t_copies, tout, tgot, h_near, y_up, y_down, y, h, 0)
    gr = Reduce(g_copies, gout, ggot, x_near, z_up, z_down, z, x, 0)

    def out_block(j):
        return lambda f, r: dot(ctx[...], big[j, f * 4 + r].reshape(512, 256))

    def out_proj_here(j):
        def wait(i, carry):
            start = pl.multiple_of(i * 1024 + j * 256, 256)
            for half in range(2):
                pltpu.make_async_copy(
                    op_hbm.at[pl.ds(half * 256, 256), pl.ds(start, 256)], big.at[j, i, half], op_sem.at[j, i, half]
                ).wait()
            return carry

        lax.fori_loop(0, 8, wait, 0)

    for j in range(4):
        out_proj_here(j)

    tr.first(0, out_block(0))
    sg.got_from_down(False)
    sg.got_from_up(False)
    dg.got_near()
    dg.got_from_down(False)
    dg.got_from_up(False)
    sg.got_from_down(True)
    sg.got_from_up(True)
    tr.first(1, out_block(1))
    tr.second(0, out_block(0))
    sg.got_far(False)
    sg.got_far(True)

    def squares(i, total):
        block = stu[i].astype(F32)
        block = block * block
        return total + block[:, 0:128] + block[:, 128:256] + block[:, 256:384] + block[:, 384:512]

    square_sum = lax.fori_loop(0, 8, squares, jnp.zeros((ROWS, 128), F32))
    inverse = lax.rsqrt(jnp.sum(square_sum, axis=1, keepdims=True) * (1.0 / 4096) + EPS)
    inv_s[...] = jnp.broadcast_to(inverse, (ROWS, 128))

    def make_normed(i, carry):
        column = pl.multiple_of(i * 512, 512)
        rows = (stu[i].astype(F32) * inv_s[:, 0:1]) * gain_ref[:, pl.ds(column, 512)]
        normed[:, pl.ds(column, 512)] = rows.astype(BF16)
        normed_t[i, 0] = rows[:, 0:256].T.astype(BF16)
        normed_t[i, 1] = rows[:, 256:512].T.astype(BF16)
        return carry

    lax.fori_loop(0, 8, make_normed, 0)

    dg.got_from_down(True)
    dg.got_from_up(True)
    dg.got_far(False)
    tr.first(2, out_block(2))
    tr.third(0, out_block(0))
    tr.second(1, out_block(1))
    dg.got_far(True)
    for k, turn, flip in ((3, 0, 0), (6, 0, 1), (8, -1, 0), (10, 1, 0), (12, -1, 1), (14, 1, 1), (15, 2, 0), (16, 2, 1)):
        from_sibling(d_other, d_copies, k, turn, flip)

    def predict(j, carry):
        pred[j] = dot(normed[...], dist[:, :, pl.ds(pl.multiple_of(j * 256, 256), 256)].reshape(4096, 256))
        return carry

    lax.fori_loop(0, 4, predict, 0)

    inv_scale = 1.0 / math.sqrt(16 * ROWS)

    def mismatch(j):
        teacher = tr.last(j, out_block(j))
        target = (ts_ref[:, j * 256 : (j + 1) * 256].astype(F32) + teacher).astype(BF16).astype(F32)
        half = (mask_ref[...] * (pred[j] - target)).astype(BF16)
        mm[:, j * 256 : (j + 1) * 256] = half
        product = half.astype(F32) * pred[j]
        rows = product[:, 0:128] + product[:, 128:256]
        rows_s[...] = rows if j == 0 else rows_s[...] + rows

    def grad_terms(j):
        mine = mm[:, j * 256 : (j + 1) * 256]

        def term(core):
            def one(i, carry):
                big[j, i, core] = (dot(normed_t[i, core], mine) * inv_scale).astype(BF16)
                return carry

            lax.fori_loop(0, 8, one, 0)

        term(1 - c)
        src = big.at[j, :, 1 - c]
        pltpu.make_async_remote_copy(
            src_ref=src, dst_ref=sib.at[j], send_sem=b_s.at[j], recv_sem=b_r.at[j],
            device_id=sibling, device_id_type=MESH,
        ).start()
        term(c)

    def sibling_done(j, send):
        src = big.at[j, :, 1 - c]
        copy = pltpu.make_async_remote_copy(
            src_ref=src, dst_ref=sib.at[j], send_sem=b_s.at[j], recv_sem=b_r.at[j],
            device_id=sibling, device_id_type=MESH,
        )
        if send:
            copy.wait_send()
        else:
            copy.wait_recv()

    def grad_block(j):
        return lambda f, r: big[j, r * 2 + f, c].astype(F32) + sib[j, r * 2 + f].astype(F32)

    def grad_last(j):
        gd_ref[:, j * 256 : (j + 1) * 256] = gr.last(j, grad_block(j)).astype(BF16)

    def grad_first(j):
        grad_terms(j)
        sibling_done(j, False)
        gr.first(j, grad_block(j))

    mismatch(0)
    grad_first(0)
    tr.first(3, out_block(3))
    tr.third(1, out_block(1))
    tr.second(2, out_block(2))
    gr.second(0, grad_block(0))
    mismatch(1)
    grad_first(1)
    tr.third(2, out_block(2))
    tr.second(3, out_block(3))
    gr.third(0, grad_block(0))
    gr.second(1, grad_block(1))
    mismatch(2)
    grad_first(2)
    tr.third(3, out_block(3))
    grad_last(0)
    gr.third(1, grad_block(1))
    gr.second(2, grad_block(2))
    mismatch(3)

    def norm_block(j):
        return lambda f, r: dot_nt(mm[...], dist[(f * 4 + r) * 2 + (j - 4)])

    i_copies = Copies(i_s, i_r)
    tr.first(4, norm_block(4))
    row_sum = jnp.broadcast_to(jnp.sum(rows_s[...], axis=1, keepdims=True), (ROWS, 128)).T[0:8]
    ims[0] = row_sum
    i_copies.start(ims.at[0], imr.at[0], 0, h_near)
    grad_first(3)
    i_copies.arrived(imr.at[0], 0, h_near)
    ims[1] = ims[0] + imr[0]
    i_copies.start(ims.at[1], imr.at[1], 1, y_up)
    i_copies.start(ims.at[1], imr.at[2], 2, y_down)
    tr.first(5, norm_block(5))
    tr.second(4, norm_block(4))
    i_copies.arrived(imr.at[1], 1, y_down)
    i_copies.arrived(imr.at[2], 2, y_up)
    i_copies.start(imr.at[1], imr.at[3], 3, y_up)
    grad_last(1)
    gr.third(2, grad_block(2))
    gr.second(3, grad_block(3))
    tr.second(5, norm_block(5))
    tr.third(4, norm_block(4))
    grad_last(2)
    gr.third(3, grad_block(3))
    i_copies.arrived(imr.at[3], 3, y_down)
    total = ims[1] + imr[1] + imr[2] + imr[3]
    inner = jnp.broadcast_to(total[0:1], (128, ROWS)).T[:, 0:1] * (1.0 / 4096)

    def stream_grad(j):
        g = j - 4
        column = pl.multiple_of(t * 512 + g * 256, 256)
        gained = tr.last(j, norm_block(j)) * gain_ref[:, pl.ds(column, 256)]
        inv = inv_s[:, 0:1]
        scaled = stu[t, :, g * 256 : (g + 1) * 256].astype(F32) * inv
        gs_ref[:, g * 256 : (g + 1) * 256] = inv * (gained - scaled * inner)

    grad_last(3)
    tr.third(5, norm_block(5))
    stream_grad(4)
    stream_grad(5)

    for copies in (kv_copies, d_copies, s_copies, i_copies):
        copies.drain()
    for j in range(4):
        sibling_done(j, True)
    tr.drain(6)
    gr.drain(4)


def body(q, k, v, out_proj, teacher_stream, student_stream, gain, distill, mask):
    anywhere = pl.BlockSpec(memory_space=pl.ANY)
    vmem = pl.BlockSpec(memory_space=pltpu.VMEM)
    sem = pltpu.SemaphoreType.DMA
    return pl.pallas_call(
        kernel,
        out_shape=(jax.ShapeDtypeStruct((256, 1024), BF16), jax.ShapeDtypeStruct((ROWS, 512), F32)),
        in_specs=[anywhere] * 4 + [vmem, anywhere, vmem, anywhere, vmem],
        out_specs=(vmem, vmem),
        scratch_shapes=[
            pltpu.VMEM((HEADS, ROWS, HEAD_DIM), BF16),
            pltpu.VMEM((2, 8, 2, ROWS, HEAD_DIM), BF16),
            pltpu.VMEM((16, 256, 1024), BF16),
            pltpu.VMEM((8, ROWS, 512), BF16),
            pltpu.VMEM((ROWS, 4096), BF16),
            pltpu.VMEM((8, 2, 256, ROWS), BF16),
            pltpu.VMEM((4, 8, 2, 256, 256), BF16),
            pltpu.VMEM((SLOTS, 7, ROWS, 256), BF16),
            pltpu.VMEM((6, 7, ROWS, 256), BF16),
            pltpu.VMEM((SLOTS, 7, 256, 256), BF16),
            pltpu.VMEM((4, 7, 256, 256), BF16),
            pltpu.VMEM((4, 8, 256, 256), BF16),
            pltpu.VMEM((4, ROWS, 256), F32),
            pltpu.VMEM((ROWS, 1024), BF16),
            pltpu.VMEM((HEADS, ROWS, HEAD_DIM), F32),
            pltpu.VMEM((HEADS, ROWS, 128), F32),
            pltpu.VMEM((HEADS, ROWS, 128), F32),
            pltpu.VMEM((ROWS, 512), BF16),
            pltpu.VMEM((ROWS, 128), F32),
            pltpu.VMEM((ROWS, 128), F32),
            pltpu.VMEM((2, 8, ROWS), F32),
            pltpu.VMEM((4, 8, ROWS), F32),
            sem((8,)), sem((4, 8, 2)),
            sem((17,)), sem((17,)), sem((17,)), sem((17,)), sem((17,)), sem((17,)),
            sem((42,)), sem((42,)), sem((28,)), sem((28,)), sem((4,)), sem((4,)), sem((4,)), sem((4,)),
        ],
        compiler_params=pltpu.CompilerParams(
            collective_id=0, has_side_effects=True, vmem_limit_bytes=63 * 2**20
        ),
        name="distill",
    )(
        q, k, v, out_proj, teacher_stream, student_stream, gain.reshape(1, 4096), distill,
        mask.astype(F32).reshape(ROWS, 1),
    )


def solution(mesh):
    placed = (
        P("seq", "tensor"),
        P("seq", "tensor"),
        P("seq", "tensor"),
        P("tensor", None),
        P("seq", "tensor"),
        P("seq", "tensor"),
        P(),
        P("seq", "tensor"),
        P("seq"),
    )
    return jax.shard_map(
        body,
        mesh=mesh,
        in_specs=placed,
        out_specs=(P("seq", "tensor"), P("seq", "tensor")),
        check_vma=False,
    )
```

time: 516 us -> 175 us (0.34)
  waiting for transfers between devices: 402 us -> 0 us
  Pallas kernels: 0 us -> 169 us
  matrix products: 70.6 us -> 0 us
  other arithmetic: 25.7 us -> 0.68 us
  between operations: 14.2 us -> 0.64 us
    reduce_scatter x2 -> x0, waiting for transfers between devices: 189 us -> none  [the longest x1 95.3 us: body(): lax.psum_scatter((lax.dot_general(normed, mismatch_half, (((0,), (0,)), (...]
    pallas_call x0 -> x1, Pallas kernels: none -> 169 us  [body(): pl.pallas_call(kernel, out_shape=(jax.ShapeDtypeStruct((256, 1024), BF16)...]
    all_gather x4 -> x0, waiting for transfers between devices: 122 us -> none  [the longest x1 49.1 us: body(): proj_full = lax.all_gather(distill_proj, 'seq', axis=0, tiled=True)]
    psum x1 -> x0, waiting for transfers between devices: 88.5 us -> none  [body(): lax.psum(normed_terms.astype(jnp.bfloat16), 'tensor').astype(jnp.float32)]
    dot_general x6 -> x0, matrix products: 70.6 us -> none  [the longest x1 17.4 us: body(): jnp.einsum('hqk,khd->hqd', weights.astype(jnp.bfloat16), values_heads, pr...]
    reduce_sum x3 -> x0, other arithmetic: 24.6 us -> none  [the longest x1 18.7 us: body(): totals = jnp.sum(weights, axis=-1)]
  transfers between devices with their start and end apart: 7 -> 0, of which waited for: 7 -> 0; matrix products, arithmetic and copies ran while one was open for 17% -> 0% of each run, Pallas kernels for 0% -> 0%
where the time goes in v1:
time: 175 us
  Pallas kernels  169 us (97%)
  local copies, waits for them, and re-layouts  4.73 us (3%)
    pallas_call x1, Pallas kernels, body(): pl.pallas_call(kernel, out_shape=(jax.ShapeDtypeStruct((256, 1024), BF16)...  169 us
    unnamed x2, local copies, waits for them, and re-layouts  3.93 us

profile of v1, /device:TPU:0, one launch (start us, length us, event | category | flops | bytes accessed | tf_op | source)
XLA Modules:
  0.0 174.6 jit_solution(10254023615403423234)
XLA Ops:
  0.6 0.7 convert_element_type.3
  1.3 0.8 reshape.12.mask_ref
  2.1 168.6 %distill.1 = (bf16[256,1024]{1,0:T(8,128)(2,1)}, f32[384,512]{1,0:T(8,128)}) custom-call(bf16[384,512]{1,0:T(8,128)(2,1)} %q_hbm.1, bf16[384,128]{1,0:T(8,128)(2,1)} %k_hbm.1, bf16[384,128]{1,0:T(8,128)(2,1)} %v_hbm.1, bf16[512,8192]{1,0:T(8,128)(2,1)} %op_hbm.1, bf16[384,1024]{1,0:T(8,128)(2,1)} %ts_ref.1, bf16[384,512]{1,0:T(8,128)(2,1)} %ss_hbm.1, ...), custom_call_target="tpu_custom_call" | custom-call | tf_op jit(solution)/shard_map/distill/pallas_call | solution.py:537
  170.7 1.9 %copy.14 = bf16[256,1024]{1,0:T(8,128)(2,1)} copy(bf16[256,1024]{1,0:T(8,128)(2,1)} %get-tuple-element.4) | data formatting | bytes 1048576
  172.6 2.1 %copy.15 = f32[384,512]{1,0:T(8,128)} copy(f32[384,512]{1,0:T(8,128)} %get-tuple-element.5) | data formatting | bytes 1572864

commit v2 on v1

v2 whole, which is shorter than its diff:
```python
import functools
import math

import jax
import jax.numpy as jnp
from jax import lax
from jax.experimental import pallas as pl
from jax.experimental.pallas import tpu as pltpu
from jax.sharding import PartitionSpec as P

HEADS = 4
HEAD_DIM = 128
EPS = 1e-05
ROWS = 384
MASKED = -1e30
MESH = pl.DeviceIdType.MESH
F32 = jnp.float32
BF16 = jnp.bfloat16


def dot(a, b):
    return jnp.dot(a, b, preferred_element_type=F32)


def dot_nt(a, b):
    return lax.dot_general(a, b, (((1,), (1,)), ((), ())), preferred_element_type=F32)


PAIR_FIRST_T = (2, 3, 5)
PAIR_FIRST_G = ()


class Copies:
    def __init__(self, send, recv):
        self.send, self.recv = send, recv
        self.started = []

    def make(self, src, dst, k, device):
        return pltpu.make_async_remote_copy(
            src_ref=src, dst_ref=dst, send_sem=self.send.at[k], recv_sem=self.recv.at[k],
            device_id=device, device_id_type=MESH,
        )

    def start(self, src, dst, k, device, again=None):
        self.make(src, dst, k, device).start()
        self.started.append((again or (lambda: src), k, device))

    def arrived(self, ref, k, device):
        self.make(ref, ref, k, device).wait_recv()

    def drain(self):
        for again, k, device in self.started:
            src = again()
            self.make(src, src, k, device).wait_send()
        self.started = []


class Gather:
    def __init__(self, copies, whole, half, near, up, down, ring, pair, other):
        self.c, self.whole, self.half = copies, whole, half
        self.near, self.up, self.down = near, up, down
        self.ring, self.pair, self.other = ring, pair, other
        self.loads = []

    def loaded(self):
        for copy in self.loads:
            copy.wait()
        self.loads = []

    def at(self, turn, flip):
        r = lax.rem(self.ring + (turn + 4), 4)
        f = 1 - self.pair if flip else self.pair
        return r, f

    def go(self, k, device, place):
        ref = self.whole(*self.at(*place))
        self.c.start(ref, ref, k, device, lambda: self.whole(*self.at(*place)))

    def go_half(self, k, device, place, part):
        ref = self.half(*self.at(*place), part)
        self.c.start(ref, ref, k, device, lambda: self.half(*self.at(*place), part))

    def across(self, k, place):
        if self.other is not None:
            self.go(k, self.other, place)

    def own_near(self):
        self.loaded()
        self.go(0, self.near, (0, False))

    def own_ring(self):
        self.loaded()
        self.go(1, self.up, (0, False))
        self.go(2, self.down, (0, False))

    def own_across(self):
        self.loaded()
        self.across(3, (0, False))

    def got_near(self):
        place = (0, True)
        self.c.arrived(self.whole(*self.at(*place)), 0, self.near)
        self.go(4, self.up, place)
        self.go(5, self.down, place)
        self.across(6, place)

    def got_from_down(self, flip):
        place = (-1, flip)
        self.c.arrived(self.whole(*self.at(*place)), 4 if flip else 1, self.down)
        self.go_half(11 if flip else 7, self.up, place, 0)
        self.across(12 if flip else 8, place)

    def got_from_up(self, flip):
        place = (1, flip)
        self.c.arrived(self.whole(*self.at(*place)), 5 if flip else 2, self.up)
        self.go_half(13 if flip else 9, self.down, place, 1)
        self.across(14 if flip else 10, place)

    def got_far(self, flip):
        place = (2, flip)
        self.c.arrived(self.half(*self.at(*place), 0), 11 if flip else 7, self.down)
        self.c.arrived(self.half(*self.at(*place), 1), 13 if flip else 9, self.up)
        self.across(16 if flip else 15, place)

    def down_own(self):
        self.got_from_down(False)

    def down_pair(self):
        self.got_from_down(True)

    def up_own(self):
        self.got_from_up(False)

    def up_pair(self):
        self.got_from_up(True)

    def far_own(self):
        self.got_far(False)

    def far_pair(self):
        self.got_far(True)


class Reduce:
    def __init__(self, copies, out, got, near, up, down, ring, pair, places):
        self.c, self.out, self.got = copies, out, got
        self.near, self.up, self.down = near, up, down
        self.ring, self.pair, self.places = ring, pair, places
        self.half = out.shape[2] // 2
        self.pending = {}

    def to(self, turn):
        return lax.rem(self.ring + (turn + 4), 4)

    def put(self, j, slot, value):
        o = self.places[j]
        for src, sem, device in self.pending.pop((o, slot), []):
            self.c.make(src, src, sem, device).wait_send()
        self.out[o, slot] = value.astype(BF16)

    def post(self, j, slot, k, device, part=None):
        rows = slice(None) if part is None else pl.ds(part * self.half, self.half)
        o, sem = self.places[j], j * 8 + k
        src = self.out.at[o, slot, rows]
        self.c.make(src, self.got.at[j, slot, rows], sem, device).start()
        self.pending.setdefault((o, slot), []).append((src, sem, device))

    def send(self, j, k, device, value):
        self.put(j, k, value)
        self.post(j, k, k, device)

    def arrived(self, j, slot, k, device, part=None):
        rows = slice(None) if part is None else pl.ds(part * self.half, self.half)
        ref = self.got.at[j, slot, rows]
        self.c.make(ref, ref, j * 8 + k, device).wait_recv()

    def load(self, j, k):
        return self.got[j, k].astype(F32)


    def first(self, j, block):
        self.send(j, 0, self.up, block(0, self.to(2)))
        self.send(j, 1, self.down, block(1, self.to(2)))
        self.send(j, 2, self.up, block(1, self.to(1)))
        self.send(j, 3, self.down, block(0, self.to(-1)))

    def second(self, j, block):
        self.arrived(j, 0, 0, self.down)
        self.send(j, 4, self.up, block(0, self.to(1)) + self.load(j, 0))
        self.arrived(j, 1, 1, self.up)
        self.send(j, 5, self.down, block(1, self.to(-1)) + self.load(j, 1))

    def total(self, j, block, f):
        return block(f, self.ring) + self.load(j, 4 - 2 * f) + self.load(j, 3 + 2 * f)

    def third(self, j, block):
        for k, device in ((2, self.down), (3, self.up), (4, self.down), (5, self.up)):
            self.arrived(j, k, k, device)
        self.send(j, 6, self.near, self.total(j, block, 1 - self.pair))

    def last(self, j, block):
        mine = self.total(j, block, self.pair)
        self.arrived(j, 6, 6, self.near)
        return mine + self.load(j, 6)


    def near_first(self, j, block):
        for r in range(4):
            self.send(j, r, self.near, block(1 - self.pair, r))

    def both(self, j, block, r):
        return block(self.pair, r) + self.load(j, r)

    def near_ring(self, j, block):
        for r in range(4):
            self.arrived(j, r, r, self.near)
        self.put(j, 4, self.both(j, block, self.to(2)))
        self.post(j, 4, 4, self.up, 0)
        self.post(j, 4, 5, self.down, 1)

    def near_second(self, j, block):
        o, n = self.places[j], self.half
        value = self.both(j, block, self.to(1))
        self.arrived(j, 4, 4, self.down, 0)
        self.put(j, 5, value)
        self.out[o, 5, 0:n] = (value[0:n] + self.got[j, 4, 0:n].astype(F32)).astype(BF16)
        self.post(j, 5, 6, self.up)
        value = self.both(j, block, self.to(-1))
        self.arrived(j, 4, 5, self.up, 1)
        self.put(j, 6, value)
        self.out[o, 6, n : 2 * n] = (value[n : 2 * n] + self.got[j, 4, n : 2 * n].astype(F32)).astype(BF16)
        self.post(j, 6, 7, self.down)

    def near_last(self, j, block):
        mine = self.both(j, block, self.ring)
        self.arrived(j, 5, 6, self.down)
        self.arrived(j, 6, 7, self.up)
        return mine + self.load(j, 5) + self.load(j, 6)

    def drain(self):
        for sent in self.pending.values():
            for src, sem, device in sent:
                self.c.make(src, src, sem, device).wait_send()
        self.pending = {}


class Group:
    def __init__(self, reduce, j, block, ready):
        self.reduce, self.j, self.block, self.ready = reduce, j, block, ready

    def first(self):
        if self.ready is not None:
            self.ready()
        self.reduce.first(self.j, self.block)

    def near_first(self):
        if self.ready is not None:
            self.ready()
        self.reduce.near_first(self.j, self.block)

    def second(self):
        self.reduce.second(self.j, self.block)

    def third(self):
        self.reduce.third(self.j, self.block)

    def near_ring(self):
        self.reduce.near_ring(self.j, self.block)

    def near_second(self):
        self.reduce.near_second(self.j, self.block)


def kernel(
    q_hbm, k_hbm, v_hbm, op_hbm, ts_hbm, ss_hbm, gain_ref, dp_hbm, mask_ref,
    gd_ref, gs_ref,
    q4, kv, dist, stu, normed, normed_t, big, tout, tgot, gout, ggot, sib,
    pred, mm, ts_ref, mask_s, acc, m_s, ctx, inv_s, rows_s, inner_s, ims, imr,
    local, op_sem, kv_s, kv_r, d_s, d_r, s_s, s_r, t_s, t_r, g_s, g_r, b_s, b_r, i_s, i_r,
):
    me, s = lax.axis_index("tensor"), lax.axis_index("seq")
    h, y = lax.div(me, 4), lax.rem(me, 4)
    z, x, c = lax.div(s, 4), lax.rem(lax.div(s, 2), 2), lax.rem(s, 2)
    p = lax.div(s, 2)

    def on_seq(zz, xx, cc):
        return {"tensor": me, "seq": zz * 4 + xx * 2 + cc}

    def on_tensor(hh, yy):
        return {"tensor": hh * 4 + yy, "seq": s}

    z_up, z_down = on_seq(lax.rem(z + 1, 4), x, c), on_seq(lax.rem(z + 3, 4), x, c)
    x_near, sibling = on_seq(z, 1 - x, c), on_seq(z, x, 1 - c)
    y_up, y_down = on_tensor(h, lax.rem(y + 1, 4)), on_tensor(h, lax.rem(y + 3, 4))
    h_near = on_tensor(1 - h, y)

    own_copies = [
        pltpu.make_async_copy(k_hbm, kv.at[0, p, c], local.at[0]),
        pltpu.make_async_copy(v_hbm, kv.at[1, p, c], local.at[1]),
        pltpu.make_async_copy(ss_hbm, stu.at[me], local.at[2]),
        pltpu.make_async_copy(dp_hbm, dist.at[s], local.at[3]),
    ] + [
        pltpu.make_async_copy(q_hbm.at[:, pl.ds(i * HEAD_DIM, HEAD_DIM)], q4.at[i], local.at[4 + i])
        for i in range(HEADS)
    ]
    for copy in own_copies:
        copy.start()

    barrier = pltpu.get_barrier_semaphore()
    for device in (z_up, z_down, x_near, sibling, y_up, y_down, h_near):
        pl.semaphore_signal(barrier, inc=1, device_id=device, device_id_type=MESH)
    pl.semaphore_wait(barrier, 7)

    kv_copies, d_copies, s_copies = Copies(kv_s, kv_r), Copies(d_s, d_r), Copies(s_s, s_r)

    def kv_gather(core):
        return Gather(
            kv_copies, lambda r, f: kv.at[:, r * 2 + f, core], lambda r, f, part: kv.at[part, r * 2 + f, core],
            x_near, z_up, z_down, z, x, sibling,
        )

    def d_gather(core):
        return Gather(
            d_copies, lambda r, f: dist.at[(r * 2 + f) * 2 + core],
            lambda r, f, part: dist.at[(r * 2 + f) * 2 + core, pl.ds(part * 128, 128)],
            x_near, z_up, z_down, z, x, sibling,
        )

    kvg, dg = kv_gather(c), d_gather(c)
    sg = Gather(
        s_copies, lambda r, f: stu.at[f * 4 + r],
        lambda r, f, part: stu.at[f * 4 + r, pl.ds(part * 192, 192)],
        h_near, y_up, y_down, y, h, None,
    )

    def from_sibling(gather, copies, k, turn, flip):
        copies.arrived(gather.whole(*gather.at(turn, flip)), k, sibling)

    kv_other, d_other = kv_gather(1 - c), d_gather(1 - c)

    kvg.loads, sg.loads, dg.loads = own_copies[0:2], own_copies[2:3], own_copies[3:4]

    def load_out_proj(i, carry):
        for j in range(4):
            start = pl.multiple_of(i * 1024 + j * 256, 256)
            for half in range(2):
                pltpu.make_async_copy(
                    op_hbm.at[pl.ds(half * 256, 256), pl.ds(start, 256)], big.at[j, i, half], op_sem.at[j, i, half]
                ).start()
        return carry

    load_stream = pltpu.make_async_copy(ts_hbm, ts_ref, local.at[8])

    def load_later():
        lax.fori_loop(0, 8, load_out_proj, 0)
        load_stream.start()
        rows_s[...] = jnp.zeros_like(rows_s)

    scale = math.log2(math.e) / math.sqrt(HEAD_DIM)

    ones = jnp.ones((2 * ROWS, HEAD_DIM), BF16)

    def keys_values(block):
        values = kv[1, block].reshape(2 * ROWS, HEAD_DIM)
        return kv[0, block].reshape(2 * ROWS, HEAD_DIM), jnp.concatenate([values, ones], axis=1)

    def own_pair():
        load_later()
        for copy in own_copies[4:]:
            copy.wait()
        from_sibling(kv_other, kv_copies, 3, 0, False)
        keys, values = keys_values(p)
        visible = (
            lax.broadcasted_iota(jnp.int32, (ROWS, 2 * ROWS), 1)
            <= lax.broadcasted_iota(jnp.int32, (ROWS, 2 * ROWS), 0) + c * ROWS
        )
        scores = dot_nt(q4[0], keys)
        for i in range(HEADS):
            following = dot_nt(q4[i + 1], keys) if i + 1 < HEADS else None
            scores = jnp.where(visible, scores * scale, MASKED)
            top = jnp.max(scores, axis=1, keepdims=True)
            weights = jnp.exp2(scores - top)
            m_s[i] = jnp.broadcast_to(top, (ROWS, 128))
            acc[i] = dot(weights.astype(BF16), values)
            scores = following

    def step(i, carry):
        turn, flip = 0, 0
        for k, (tasks, (copy, turn_k, flip_k)) in enumerate(attended):
            @pl.when(i == k)
            def _(tasks=tasks, copy=copy, turn_k=turn_k, flip_k=flip_k):
                for task in tasks:
                    task()
                from_sibling(kv_other, kv_copies, copy, turn_k, flip_k)

            turn = jnp.where(i == k, turn_k % 4, turn)
            flip = jnp.where(i == k, int(flip_k), flip)
        block = lax.rem(z + turn, 4) * 2 + x * (1 - flip) + (1 - x) * flip

        @pl.when(block < p)
        def _():
            keys, values = keys_values(block)
            scores = dot_nt(q4[0], keys)
            for i in range(HEADS):
                following = dot_nt(q4[i + 1], keys) if i + 1 < HEADS else None
                before = m_s[i, :, 0:1]
                top = jnp.maximum(before, jnp.max(scores, axis=1, keepdims=True) * scale)
                weights = jnp.exp2(scores * scale - top)
                m_s[i] = jnp.broadcast_to(top, (ROWS, 128))
                acc[i] = acc[i] * jnp.exp2(before - top) + dot(weights.astype(BF16), values)
                scores = following

        return carry

    t_copies, g_copies = Copies(t_s, t_r), Copies(g_s, g_r)
    tr = Reduce(t_copies, tout, tgot, h_near, y_up, y_down, y, h, (0, 1, 2, 0, 1, 2))
    gr = Reduce(g_copies, gout, ggot, x_near, z_up, z_down, z, x, (0, 1, 0, 1))

    def out_block(j):
        return lambda f, r: dot(ctx[...], big[j, f * 4 + r].reshape(512, 256))

    def out_proj_here(j):
        def wait(i, carry):
            start = pl.multiple_of(i * 1024 + j * 256, 256)
            for half in range(2):
                pltpu.make_async_copy(
                    op_hbm.at[pl.ds(half * 256, 256), pl.ds(start, 256)], big.at[j, i, half], op_sem.at[j, i, half]
                ).wait()
            return carry

        lax.fori_loop(0, 8, wait, 0)

    def finish_context():
        for i in range(HEADS):
            ctx[:, i * HEAD_DIM : (i + 1) * HEAD_DIM] = (acc[i, :, 0:HEAD_DIM] / acc[i, :, HEAD_DIM:]).astype(BF16)
        for j in range(4):
            out_proj_here(j)
        load_stream.wait()
        for i in range(3):
            row = mask_ref[i : i + 1, :].astype(F32)
            mask_s[i * 128 : (i + 1) * 128, :] = jnp.broadcast_to(row, (128, 128)).T

    def squares(i, total):
        block = stu[i].astype(F32)
        block = block * block
        return total + block[:, 0:128] + block[:, 128:256] + block[:, 256:384] + block[:, 384:512]

    def make_normed(i, carry):
        column = pl.multiple_of(i * 512, 512)
        rows = (stu[i].astype(F32) * inv_s[:, 0:1]) * gain_ref[:, pl.ds(column, 512)]
        normed[:, pl.ds(column, 512)] = rows.astype(BF16)
        normed_t[i, 0] = rows[:, 0:256].T.astype(BF16)
        normed_t[i, 1] = rows[:, 256:512].T.astype(BF16)
        return carry

    def normalise():
        square_sum = lax.fori_loop(0, 8, squares, jnp.zeros((ROWS, 128), F32))
        inverse = lax.rsqrt(jnp.sum(square_sum, axis=1, keepdims=True) * (1.0 / 4096) + EPS)
        inv_s[...] = jnp.broadcast_to(inverse, (ROWS, 128))
        lax.fori_loop(0, 8, make_normed, 0)

    def predict(j, carry):
        pred[j] = dot(normed[...], dist[:, :, pl.ds(pl.multiple_of(j * 256, 256), 256)].reshape(4096, 256))
        return carry

    def predict_all():
        for k, turn, flip in (
            (3, 0, 0), (6, 0, 1), (8, -1, 0), (10, 1, 0), (12, -1, 1), (14, 1, 1), (15, 2, 0), (16, 2, 1)
        ):
            from_sibling(d_other, d_copies, k, turn, flip)
        lax.fori_loop(0, 4, predict, 0)

    inv_scale = 1.0 / math.sqrt(16 * ROWS)

    def mismatch(j):
        teacher = (tr.near_last if j in PAIR_FIRST_T else tr.last)(j, out_block(j))
        target = (ts_ref[:, j * 256 : (j + 1) * 256].astype(F32) + teacher).astype(BF16).astype(F32)
        half = (mask_s[:, 0:1] * (pred[j] - target)).astype(BF16)
        mm[:, j * 256 : (j + 1) * 256] = half
        product = half.astype(F32) * pred[j]
        rows = product[:, 0:128] + product[:, 128:256]
        rows_s[...] = rows_s[...] + rows

    def grad_terms(j):
        mine = mm[:, j * 256 : (j + 1) * 256]

        def term(core):
            rows = normed_t[:, core].reshape(2048, ROWS)
            big[j, :, core] = (dot(rows, mine) * inv_scale).astype(BF16).reshape(8, 256, 256)

        term(1 - c)
        src = big.at[j, :, 1 - c]
        pltpu.make_async_remote_copy(
            src_ref=src, dst_ref=sib.at[j], send_sem=b_s.at[j], recv_sem=b_r.at[j],
            device_id=sibling, device_id_type=MESH,
        ).start()
        term(c)

    def sibling_done(j, send):
        src = big.at[j, :, 1 - c]
        copy = pltpu.make_async_remote_copy(
            src_ref=src, dst_ref=sib.at[j], send_sem=b_s.at[j], recv_sem=b_r.at[j],
            device_id=sibling, device_id_type=MESH,
        )
        if send:
            copy.wait_send()
        else:
            copy.wait_recv()

    def grad_block(j):
        return lambda f, r: big[j, r * 2 + f, c].astype(F32) + sib[j, r * 2 + f].astype(F32)

    def grad_last(j):
        last = gr.near_last if j in PAIR_FIRST_G else gr.last
        gd_ref[:, j * 256 : (j + 1) * 256] = last(j, grad_block(j)).astype(BF16)

    def norm_block(j):
        return lambda f, r: dot_nt(mm[...], dist[(f * 4 + r) * 2 + (j - 4)])

    i_copies = Copies(i_s, i_r)

    def sum_rows():
        ims[0] = jnp.broadcast_to(jnp.sum(rows_s[...], axis=1, keepdims=True), (ROWS, 128)).T[0:8]
        i_copies.start(ims.at[0], imr.at[0], 0, h_near)

    def sum_pair():
        i_copies.arrived(imr.at[0], 0, h_near)
        ims[1] = ims[0] + imr[0]
        i_copies.start(ims.at[1], imr.at[1], 1, y_up)
        i_copies.start(ims.at[1], imr.at[2], 2, y_down)

    def sum_far():
        i_copies.arrived(imr.at[1], 1, y_down)
        i_copies.arrived(imr.at[2], 2, y_up)
        i_copies.start(imr.at[1], imr.at[3], 3, y_up)

    def sum_all():
        i_copies.arrived(imr.at[3], 3, y_down)
        total = ims[1] + imr[1] + imr[2] + imr[3]
        inner = jnp.broadcast_to(total[0:1], (128, ROWS)).T[:, 0:1] * (1.0 / 4096)
        inner_s[...] = jnp.broadcast_to(inner, (ROWS, 128))

    def stream_grad(j):
        part = j - 4
        column = pl.multiple_of(me * 512 + part * 256, 256)
        gained = (tr.near_last if j in PAIR_FIRST_T else tr.last)(j, norm_block(j)) * gain_ref[:, pl.ds(column, 256)]
        inv = inv_s[:, 0:1]
        scaled = stu[me, :, part * 256 : (part + 1) * 256].astype(F32) * inv
        gs_ref[:, part * 256 : (part + 1) * 256] = inv * (gained - scaled * inner_s[:, 0:1])

    t = [Group(tr, j, (out_block if j < 4 else norm_block)(j), None) for j in range(6)]
    g = [Group(gr, j, grad_block(j), functools.partial(sibling_done, j, False)) for j in range(4)]
    mis = [functools.partial(mismatch, j) for j in range(4)]
    terms = [functools.partial(grad_terms, j) for j in range(4)]
    grad_out = [functools.partial(grad_last, j) for j in range(4)]
    stream_out = [functools.partial(stream_grad, j) for j in (4, 5)]
    near, far, far_pair = (6, 0, True), (15, 2, False), (16, 2, True)
    down, up, down_pair, up_pair = (8, -1, False), (10, 1, False), (12, -1, True), (14, 1, True)

    for task in (
        kvg.own_near, sg.own_ring, kvg.own_across, kvg.own_ring, own_pair, sg.own_near, kvg.got_near,
    ):
        task()
    attended = (
        ((), near),
        ((kvg.up_own, sg.down_own, sg.up_own, dg.own_across, kvg.down_own), up),
        ((kvg.up_pair, kvg.down_pair, dg.own_near), down),
        ((dg.own_ring, kvg.far_own, sg.got_near), up_pair),
        ((), far),
        ((kvg.far_pair,), down_pair),
        ((), far_pair),
    )
    lax.fori_loop(0, 7, step, 0)
    for task in (
        finish_context, t[2].near_first, t[1].first, t[0].first, sg.up_pair, sg.far_own, dg.got_near, dg.down_pair,
        dg.up_pair, t[3].near_first, sg.down_pair, dg.up_own, dg.down_own, t[2].near_ring, t[0].second, dg.far_pair,
        t[2].near_second, dg.far_own, sg.far_pair, normalise, t[1].second, t[0].third, predict_all, t[3].near_ring,
        mis[2], terms[2], t[1].third, t[3].near_second, g[2].first, mis[0], terms[0], mis[1], g[0].first, mis[3],
        t[5].near_first, g[2].second, t[4].first, terms[1], g[1].first, terms[3], g[3].first, sum_rows, g[0].second,
        t[4].second, g[2].third, sum_pair, t[4].third, t[5].near_ring, sum_far, g[1].second, g[0].third, g[3].second,
        sum_all, g[1].third, t[5].near_second, grad_out[2], g[3].third, grad_out[0], stream_out[0], stream_out[1],
        grad_out[1], grad_out[3],
    ):
        task()

    for copies in (kv_copies, d_copies, s_copies, i_copies):
        copies.drain()
    for j in range(4):
        sibling_done(j, True)
    tr.drain()
    gr.drain()


def body(q, k, v, out_proj, teacher_stream, student_stream, gain, distill, mask):
    anywhere = pl.BlockSpec(memory_space=pl.ANY)
    vmem = pl.BlockSpec(memory_space=pltpu.VMEM)
    sem = pltpu.SemaphoreType.DMA
    return pl.pallas_call(
        kernel,
        out_shape=(jax.ShapeDtypeStruct((256, 1024), BF16), jax.ShapeDtypeStruct((ROWS, 512), F32)),
        in_specs=[anywhere] * 6 + [vmem, anywhere, vmem],
        out_specs=(vmem, vmem),
        scratch_shapes=[
            pltpu.VMEM((HEADS, ROWS, HEAD_DIM), BF16),
            pltpu.VMEM((2, 8, 2, ROWS, HEAD_DIM), BF16),
            pltpu.VMEM((16, 256, 1024), BF16),
            pltpu.VMEM((8, ROWS, 512), BF16),
            pltpu.VMEM((ROWS, 4096), BF16),
            pltpu.VMEM((8, 2, 256, ROWS), BF16),
            pltpu.VMEM((4, 8, 2, 256, 256), BF16),
            pltpu.VMEM((3, 7, ROWS, 256), BF16),
            pltpu.VMEM((6, 7, ROWS, 256), BF16),
            pltpu.VMEM((2, 7, 256, 256), BF16),
            pltpu.VMEM((4, 7, 256, 256), BF16),
            pltpu.VMEM((4, 8, 256, 256), BF16),
            pltpu.VMEM((4, ROWS, 256), F32),
            pltpu.VMEM((ROWS, 1024), BF16),
            pltpu.VMEM((ROWS, 1024), BF16),
            pltpu.VMEM((ROWS, 128), F32),
            pltpu.VMEM((HEADS, ROWS, 2 * HEAD_DIM), F32),
            pltpu.VMEM((HEADS, ROWS, 128), F32),
            pltpu.VMEM((ROWS, 512), BF16),
            pltpu.VMEM((ROWS, 128), F32),
            pltpu.VMEM((ROWS, 128), F32),
            pltpu.VMEM((ROWS, 128), F32),
            pltpu.VMEM((2, 8, ROWS), F32),
            pltpu.VMEM((4, 8, ROWS), F32),
            sem((9,)), sem((4, 8, 2)),
            sem((17,)), sem((17,)), sem((17,)), sem((17,)), sem((17,)), sem((17,)),
            sem((48,)), sem((48,)), sem((32,)), sem((32,)), sem((4,)), sem((4,)), sem((4,)), sem((4,)),
        ],
        compiler_params=pltpu.CompilerParams(
            collective_id=0, has_side_effects=True, vmem_limit_bytes=65400 * 1024
        ),
        name="distill",
    )(
        q, k, v, out_proj, teacher_stream, student_stream, gain.reshape(1, 4096), distill,
        mask.reshape(3, 128),
    )


def solution(mesh):
    placed = (
        P("seq", "tensor"),
        P("seq", "tensor"),
        P("seq", "tensor"),
        P("tensor", None),
        P("seq", "tensor"),
        P("seq", "tensor"),
        P(),
        P("seq", "tensor"),
        P("seq"),
    )
    return jax.shard_map(
        body,
        mesh=mesh,
        in_specs=placed,
        out_specs=(P("seq", "tensor"), P("seq", "tensor")),
        check_vma=False,
    )
```

time: 175 us -> 128 us (0.73)
  Pallas kernels: 169 us -> 124 us
    pallas_call x1, Pallas kernels: 169 us -> 124 us  [body(): pl.pallas_call(kernel, out_shape=(jax.ShapeDtypeStruct((256, 1024), BF16)...]
where the time goes in v2:
time: 128 us
  Pallas kernels  124 us (97%)
  local copies, waits for them, and re-layouts  3.93 us (3%)
    pallas_call x1, Pallas kernels, body(): pl.pallas_call(kernel, out_shape=(jax.ShapeDtypeStruct((256, 1024), BF16)...  124 us
    unnamed x2, local copies, waits for them, and re-layouts  3.93 us

profile of v2, /device:TPU:0, one launch (start us, length us, event | category | flops | bytes accessed | tf_op | source)
XLA Modules:
  0.0 128.2 jit_solution(3465902363023194041)
XLA Ops:
  0.6 123.6 %distill.1 = (bf16[256,1024]{1,0:T(8,128)(2,1)}, f32[384,512]{1,0:T(8,128)}) custom-call(bf16[384,512]{1,0:T(8,128)(2,1)} %q_hbm.1, bf16[384,128]{1,0:T(8,128)(2,1)} %k_hbm.1, bf16[384,128]{1,0:T(8,128)(2,1)} %v_hbm.1, bf16[512,8192]{1,0:T(8,128)(2,1)} %op_hbm.1, bf16[384,1024]{1,0:T(8,128)(2,1)} %ts_hbm.1, bf16[384,512]{1,0:T(8,128)(2,1)} %ss_hbm.1, ...), custom_call_target="tpu_custom_call" | custom-call | tf_op jit(solution)/shard_map/distill/pallas_call | solution.py:598
  124.2 1.9 %copy.13 = bf16[256,1024]{1,0:T(8,128)(2,1)} copy(bf16[256,1024]{1,0:T(8,128)(2,1)} %get-tuple-element.4) | data formatting | bytes 1048576
  126.1 2.1 %copy.14 = f32[384,512]{1,0:T(8,128)} copy(f32[384,512]{1,0:T(8,128)} %get-tuple-element.5) | data formatting | bytes 1572864

commit v3 on v2

--- a/solution.py
+++ b/solution.py
@@ -340,13 +340,13 @@
 
     kvg.loads, sg.loads, dg.loads = own_copies[0:2], own_copies[2:3], own_copies[3:4]
 
+    def weight_copy(j, i):
+        start = pl.multiple_of(i * 1024 + j * 256, 256)
+        return pltpu.make_async_copy(op_hbm.at[:, :, pl.ds(start, 256)], big.at[j, i], op_sem.at[j, i])
+
     def load_out_proj(i, carry):
         for j in range(4):
-            start = pl.multiple_of(i * 1024 + j * 256, 256)
-            for half in range(2):
-                pltpu.make_async_copy(
-                    op_hbm.at[pl.ds(half * 256, 256), pl.ds(start, 256)], big.at[j, i, half], op_sem.at[j, i, half]
-                ).start()
+            weight_copy(j, i).start()
         return carry
 
     load_stream = pltpu.make_async_copy(ts_hbm, ts_ref, local.at[8])
@@ -365,7 +365,6 @@
         return kv[0, block].reshape(2 * ROWS, HEAD_DIM), jnp.concatenate([values, ones], axis=1)
 
     def own_pair():
-        load_later()
         for copy in own_copies[4:]:
             copy.wait()
         from_sibling(kv_other, kv_copies, 3, 0, False)
@@ -383,6 +382,7 @@
             m_s[i] = jnp.broadcast_to(top, (ROWS, 128))
             acc[i] = dot(weights.astype(BF16), values)
             scores = following
+        load_later()
 
     def step(i, carry):
         turn, flip = 0, 0
@@ -421,11 +421,7 @@
 
     def out_proj_here(j):
         def wait(i, carry):
-            start = pl.multiple_of(i * 1024 + j * 256, 256)
-            for half in range(2):
-                pltpu.make_async_copy(
-                    op_hbm.at[pl.ds(half * 256, 256), pl.ds(start, 256)], big.at[j, i, half], op_sem.at[j, i, half]
-                ).wait()
+            weight_copy(j, i).wait()
             return carry
 
         lax.fori_loop(0, 8, wait, 0)
@@ -625,7 +621,7 @@
             pltpu.VMEM((ROWS, 128), F32),
             pltpu.VMEM((2, 8, ROWS), F32),
             pltpu.VMEM((4, 8, ROWS), F32),
-            sem((9,)), sem((4, 8, 2)),
+            sem((9,)), sem((4, 8)),
             sem((17,)), sem((17,)), sem((17,)), sem((17,)), sem((17,)), sem((17,)),
             sem((48,)), sem((48,)), sem((32,)), sem((32,)), sem((4,)), sem((4,)), sem((4,)), sem((4,)),
         ],
@@ -634,7 +630,7 @@
         ),
         name="distill",
     )(
-        q, k, v, out_proj, teacher_stream, student_stream, gain.reshape(1, 4096), distill,
+        q, k, v, out_proj.reshape(2, 256, 8192), teacher_stream, student_stream, gain.reshape(1, 4096), distill,
         mask.reshape(3, 128),
     )
 

time: 128 us -> 129 us (level)
  no operation moved by 1% of the time
where the time goes in v3:
time: 129 us; the launch traced here: 128 us
  Pallas kernels  124 us (96%)
  local copies, waits for them, and re-layouts  3.93 us (3%)
    pallas_call x1, Pallas kernels, body(): pl.pallas_call(kernel, out_shape=(jax.ShapeDtypeStruct((256, 1024), BF16)...  124 us
    unnamed x2, local copies, waits for them, and re-layouts  3.93 us

profile of v3, /device:TPU:0, one launch (start us, length us, event | category | flops | bytes accessed | tf_op | source)
XLA Modules:
  0.0 128.4 jit_solution(1332718739251684396)
XLA Ops:
  0.6 123.9 %distill.1 = (bf16[256,1024]{1,0:T(8,128)(2,1)}, f32[384,512]{1,0:T(8,128)}) custom-call(bf16[384,512]{1,0:T(8,128)(2,1)} %q_hbm.1, bf16[384,128]{1,0:T(8,128)(2,1)} %k_hbm.1, bf16[384,128]{1,0:T(8,128)(2,1)} %v_hbm.1, bf16[2,256,8192]{2,1,0:T(8,128)(2,1)} %bitcast.3, bf16[384,1024]{1,0:T(8,128)(2,1)} %ts_hbm.1, bf16[384,512]{1,0:T(8,128)(2,1)} %ss_hbm.1, ...), custom_call_target="tpu_custom_call" | custom-call | tf_op jit(solution)/shard_map/distill/pallas_call | solution.py:594
  124.5 1.9 %copy.13 = bf16[256,1024]{1,0:T(8,128)(2,1)} copy(bf16[256,1024]{1,0:T(8,128)(2,1)} %get-tuple-element.4) | data formatting | bytes 1048576
  126.4 2.1 %copy.14 = f32[384,512]{1,0:T(8,128)} copy(f32[384,512]{1,0:T(8,128)} %get-tuple-element.5) | data formatting | bytes 1572864
